TPU v7x, 32 devices: a whole 2x2x4 slice. The times are simulated.
32 devices in a mesh: groups: 2 (over x), row: 16 (over z, y, core).
Axes of the slice: x: 2, y: 2, z: 4, core: 2. Of those that a mesh axis runs over, the one named last changes fastest.
Arguments:
- gate_pre: bfloat16 [4096, 14336], P(('groups', 'row')), parts along dimension 0, may hold values from -8 to 8
- up_pre: bfloat16 [4096, 14336], P(('groups', 'row')), parts along dimension 0, may hold values from -6 to 6
- out_grad: bfloat16 [4096, 4096], P(('groups', 'row')), parts along dimension 0, may hold values from -6 to 6
- down_weight: bfloat16 [14336, 4096], P('row'), may hold values from -0.046875 to 0.046875
Outputs:
- weight_grad: bfloat16 [28672, 4096], P(('groups', 'row')), parts along dimension 0
- gate_grad: bfloat16 [4096, 14336], P(('groups', 'row')), parts along dimension 0
- up_grad: bfloat16 [4096, 14336], P(('groups', 'row')), parts along dimension 0
There are 2 independent parts, one for each index of `groups`. A program takes and returns all parts, laid end to end along the dimension named above; an argument that names none is the same for every part. Nothing has to cross between parts.
All inputs are finite; a program needn't handle non-finite values.
Results may differ from a plain program's by a relative error of at most 0.005.
Values may be sent and summed in bfloat16 or wider, within the bound.
A program may use at most 128 MiB of HBM per device.

v0:
```python
import jax
import jax.numpy as jnp
from jax import lax
from jax.sharding import PartitionSpec as P


def local(gate_pre, up_pre, out_grad, down_weight):
    gate_wide = gate_pre.astype(jnp.float32)
    up_wide = up_pre.astype(jnp.float32)
    hidden = (jax.nn.silu(gate_wide) * up_wide).astype(jnp.bfloat16)
    hidden_cols = lax.all_to_all(hidden, "row", split_axis=1, concat_axis=0, tiled=True)
    grads_all = lax.all_gather(out_grad, "row", axis=0, tiled=True)
    weight_acc = lax.dot_general(
        hidden_cols, grads_all, (((0,), (0,)), ((), ())), preferred_element_type=jnp.float32
    )
    grad_cols = lax.dot_general(
        grads_all, down_weight, (((1,), (1,)), ((), ())), preferred_element_type=jnp.float32
    ).astype(jnp.bfloat16)
    weight_grad = weight_acc.astype(jnp.bfloat16)
    grad_rows = lax.all_to_all(grad_cols, "row", split_axis=0, concat_axis=1, tiled=True)
    grad_wide = grad_rows.astype(jnp.float32)
    sigmoid = 1.0 / (1.0 + jnp.exp(-gate_wide))
    up_grad = (grad_wide * gate_wide * sigmoid).astype(jnp.bfloat16)
    gate_grad = (grad_wide * up_wide * sigmoid * (1.0 + gate_wide * (1.0 - sigmoid))).astype(
        jnp.bfloat16
    )
    return (weight_grad, gate_grad, up_grad)


def solution(mesh):
    return jax.shard_map(
        local,
        mesh=mesh,
        in_specs=(
            P(("groups", "row"), None),
            P(("groups", "row"), None),
            P(("groups", "row"), None),
            P("row", None),
        ),
        out_specs=(
            P(("groups", "row"), None),
            P(("groups", "row"), None),
            P(("groups", "row"), None),
        ),
        check_vma=False,
    )
```

profile of v0, /device:TPU:13, one launch (start us, length us, event | category | flops | bytes accessed | tf_op | source)
XLA Modules:
  0.0 393.4 jit_solution(9885769025215370310)
XLA Ops:
  7.2 0.0 all-gather.2.cloned.1.call-start
  7.2 0.7 all-gather.2.cloned.1.call-update
  7.9 127.9 %all-gather.2.cloned.1.call-done = bf16[2048,4096]{1,0:T(8,128)(2,1)} async-done(((bf16[128,4096]{1,0:T(8,128)(2,1)}), bf16[2048,4096]{1,0:T(8,128)(2,1)}) %all-gather.2.cloned.1.call-update) | async-done | bytes 16777232 | tf_op jit(solution)/shard_map/all_gather | solution.py:12
  135.8 23.4 %convolution_convert_fusion.1 = bf16[2048,896]{1,0:T(8,128)(2,1)} fusion(bf16[2048,4096]{1,0:T(8,128)(2,1)} %all-gather.2.cloned.1.call-done, bf16[896,4096]{1,0:T(8,128)(2,1)} %param.7), kind=kOutput, calls=%fused_computation.18 | convolution fusion | flops 15034220544 | bytes 27787264 | tf_op jit(solution)/shard_map/dot_general | solution.py:16
  159.2 7.6 %all-to-all-start.1 = ((bf16[16,128,896]{2,1,0:T(8,128)(2,1)}), bf16[16,128,896]{2,1,0:T(8,128)(2,1)}, u32[]{:S(2)}, u32[]{:S(2)}) async-start(bf16[16,128,896]{2,1,0:T(8,128)(2,1)} %bitcast.14), calls=%async_computation.1 | async-start | bytes 7340032 | tf_op jit(solution)/shard_map/all_to_all | solution.py:20
  166.7 6.0 %copy.9 = bf16[128,14336]{0,1:T(8,128)(2,1)} copy(bf16[128,14336]{1,0:T(8,128)(2,1)} %param.4) | data formatting | bytes 7340032 | tf_op args[0]
  172.8 6.1 %copy.10 = bf16[128,14336]{0,1:T(8,128)(2,1)} copy(bf16[128,14336]{1,0:T(8,128)(2,1)} %param.5) | data formatting | bytes 7340032 | tf_op args[1]
  178.8 69.2 %all-to-all-done.1 = bf16[16,128,896]{2,1,0:T(8,128)(2,1)} async-done(((bf16[16,128,896]{2,1,0:T(8,128)(2,1)}), bf16[16,128,896]{2,1,0:T(8,128)(2,1)}, u32[]{:S(2)}, u32[]{:S(2)}) %all-to-all-start.1) | async-done | bytes 3670048 | tf_op jit(solution)/shard_map/all_to_all | solution.py:20
  248.0 5.9 %convert_bitcast_fusion = f32[128,16,896]{2,0,1:T(8,128)} fusion(bf16[16,128,896]{2,1,0:T(8,128)(2,1)} %all-to-all-done.1), kind=kLoop, calls=%fused_computation.16 | loop fusion | flops 1835008 | bytes 11010048 | tf_op jit(solution)/shard_map/convert_element_type | solution.py:21
  253.9 8.6 %copy.12 = f32[128,16,896]{0,2,1:T(8,128)} copy(f32[128,16,896]{2,0,1:T(8,128)} %convert_bitcast_fusion) | data formatting | bytes 14680064 | tf_op jit(solution)/shard_map/convert_element_type | solution.py:21
  262.4 10.0 %fusion.9 = (bf16[128,14336]{0,1:T(8,128)(2,1)}, bf16[128,14336]{0,1:T(8,128)(2,1)}, bf16[128,14336]{0,1:T(8,128)(2,1)}) fusion(bf16[128,14336]{0,1:T(8,128)(2,1)} %copy.9, f32[128,16,896]{0,2,1:T(8,128)} %copy.12, bf16[128,14336]{0,1:T(8,128)(2,1)} %copy.10), kind=kLoop, calls=%fused_computation.15 | loop fusion | flops 33030144 | bytes 25690112 | tf_op jit(solution)/shard_map/convert_element_type | solution.py:23
  272.4 4.9 %all-to-all-start = ((bf16[128,16,896]{0,2,1:T(8,128)(2,1)}), bf16[128,16,896]{0,2,1:T(8,128)(2,1)}, u32[]{:S(2)}, u32[]{:S(2)}) async-start(bf16[128,16,896]{0,2,1:T(8,128)(2,1)} %bitcast.13), calls=%async_computation | async-start | bytes 7340032 | tf_op jit(solution)/shard_map/all_to_all | solution.py:11
  277.3 6.1 %copy.14 = bf16[128,14336]{1,0:T(8,128)(2,1)} copy(bf16[128,14336]{0,1:T(8,128)(2,1)} %get-tuple-element.6) | data formatting | bytes 7340032
  283.4 6.1 %copy.13 = bf16[128,14336]{1,0:T(8,128)(2,1)} copy(bf16[128,14336]{0,1:T(8,128)(2,1)} %get-tuple-element.7) | data formatting | bytes 7340032
  289.5 69.1 %all-to-all-done = bf16[128,16,896]{0,2,1:T(8,128)(2,1)} async-done(((bf16[128,16,896]{0,2,1:T(8,128)(2,1)}), bf16[128,16,896]{0,2,1:T(8,128)(2,1)}, u32[]{:S(2)}, u32[]{:S(2)}) %all-to-all-start) | async-done | bytes 3670048 | tf_op jit(solution)/shard_map/all_to_all | solution.py:11
  358.5 6.1 %copy.11 = bf16[16,128,896]{2,1,0:T(8,128)(2,1)} copy(bf16[16,128,896]{1,2,0:T(8,128)(2,1)} %bitcast.1) | data formatting | bytes 7340032 | tf_op jit(solution)/shard_map/all_to_all | solution.py:11
  364.6 22.0 %convolution_convert_fusion = bf16[896,4096]{1,0:T(8,128)(2,1)} fusion(bf16[2048,896]{1,0:T(8,128)(2,1)} %bitcast.15, bf16[2048,4096]{1,0:T(8,128)(2,1)} %all-gather.2.cloned.1.call-done), kind=kOutput, calls=%fused_computation.17 | convolution fusion | flops 15036055552 | bytes 27787264 | tf_op jit(solution)/shard_map/dot_general | solution.py:13
Async XLA Ops:
  7.2 128.6 %all-gather.2.cloned.1.call-start = ((), (), s32[]{:S(2)}) async-start(), calls=%async_computation.2 | async-start | bytes 17825792 | tf_op jit(solution)/shard_map/all_gather | solution.py:12
  159.2 88.8 %all-to-all-start.1 = ((bf16[16,128,896]{2,1,0:T(8,128)(2,1)}), bf16[16,128,896]{2,1,0:T(8,128)(2,1)}, u32[]{:S(2)}, u32[]{:S(2)}) async-start(bf16[16,128,896]{2,1,0:T(8,128)(2,1)} %bitcast.14), calls=%async_computation.1 | async-start | bytes 7340032 | tf_op jit(solution)/shard_map/all_to_all | solution.py:20
  272.4 86.1 %all-to-all-start = ((bf16[128,16,896]{0,2,1:T(8,128)(2,1)}), bf16[128,16,896]{0,2,1:T(8,128)(2,1)}, u32[]{:S(2)}, u32[]{:S(2)}) async-start(bf16[128,16,896]{0,2,1:T(8,128)(2,1)} %bitcast.13), calls=%async_computation | async-start | bytes 7340032 | tf_op jit(solution)/shard_map/all_to_all | solution.py:11
Sparse Core Ops, SparseCore 0:
  10.2 125.5 all-gather.1
where the time goes:
time: 394 us; the launch traced here: 393 us
  waiting for transfers between devices  267 us (68%)
  matrix products  45.4 us (12%)
  local copies, waits for them, and re-layouts  38.9 us (10%)
  other arithmetic  15.9 us (4%)
  between operations  14 us (4%)
  starting transfers between devices  12.5 us (3%)
    all_gather x1, waiting for transfers between devices, local(): grads_all = lax.all_gather(out_grad, 'row', axis=0, tiled=True)  128 us
    all_to_all x1, waiting for transfers between devices, local(): lax.all_to_all(grad_cols, 'row', split_axis=0, concat_axis=1, tiled=True)  69.2 us
    all_to_all x1, waiting for transfers between devices, local(): lax.all_to_all(hidden, 'row', split_axis=1, concat_axis=0, tiled=True)  69.1 us
    unnamed x4, local copies, waits for them, and re-layouts  24.2 us
    dot_general x1, matrix products, local(): lax.dot_general(grads_all, down_weight, (((1,), (1,)), ((), ())), preferr...  23.4 us
    dot_general x1, matrix products, local(): lax.dot_general(hidden_cols, grads_all, (((0,), (0,)), ((), ())), preferr...  22 us
    convert_element_type x1, other arithmetic, local(): up_grad = (grad_wide * gate_wide * sigmoid).astype(jnp.bfloat16)  9.98 us
    convert_element_type x1, local copies, waits for them, and re-layouts, local(): grad_wide = grad_rows.astype(jnp.float32)  8.57 us
  transfers between devices with their start and end apart: 3, of which 3 were waited for; matrix products, arithmetic and copies ran while one was open for 6% of the time, Pallas kernels for 0%

commit v1 on v0

v1 whole, which is shorter than its diff:
```python
import functools

import jax
import jax.numpy as jnp
from jax import lax
from jax.experimental import pallas as pl
from jax.experimental.pallas import tpu as pltpu
from jax.sharding import PartitionSpec as P

MESH = pl.DeviceIdType.MESH
TILE = 256


def cols(ref, at, ff):
    if len(ref.shape) == 3:
        return ref.at[at]
    return ref.at[:, pl.ds(pl.multiple_of(at * ff, 128), ff)]


def kernel(
    A, B, hid_ref, og_ref, w_ref, wg_ref, gr_ref, og_all, w_v, hid_v, hid_t, gcols, wg_v,
    local_sem, ag_recv, z_send, y_send, c_send, h_send, h_recv, g_send, g_recv, out_sem,
):
    n = A * B * 2
    ff, depth = w_ref.shape
    rows = og_ref.shape[0]
    me = lax.axis_index("row")
    z, y, c = me // (2 * B), (me // 2) % B, me % 2

    def idx(zz, yy, cc):
        return (zz * B + yy) * 2 + cc

    own_og = pltpu.make_async_copy(og_ref, og_all.at[me], local_sem.at[0])
    own_w = pltpu.make_async_copy(w_ref, w_v, local_sem.at[1])
    own_hid = pltpu.make_async_copy(cols(hid_ref, me, ff), hid_v.at[me], local_sem.at[2])
    own_grad = pltpu.make_async_copy(gcols.at[me], cols(gr_ref, me, ff), local_sem.at[3])
    own_og.start()
    own_w.start()
    own_hid.start()

    barrier = pltpu.get_barrier_semaphore()

    @pl.loop(1, n)
    def _(k):
        pl.semaphore_signal(barrier, inc=1, device_id={"row": (me + k) % n}, device_id_type=MESH)

    pl.semaphore_wait(barrier, n - 1)

    def shard_copy(owner, target, send):
        return pltpu.make_async_remote_copy(
            og_all.at[owner], og_all.at[owner], send, ag_recv.at[owner],
            device_id={"row": target}, device_id_type=MESH,
        )

    def down(zp):
        return shard_copy(idx(zp, y, c), idx((z + A - 1) % A, y, c), z_send.at[zp])

    def up(zp):
        return shard_copy(idx(zp, y, c), idx((z + 1) % A, y, c), z_send.at[A + zp])

    def across(zp):
        return shard_copy(idx(zp, y, c), idx(z, (y + 1) % B, c), y_send.at[zp])

    def beside(zp, yp):
        return shard_copy(idx(zp, yp, c), idx(z, y, 1 - c), c_send.at[zp * B + yp])

    def hidden_copy(k):
        to = (me + k) % n
        return pltpu.make_async_remote_copy(
            cols(hid_ref, to, ff), hid_v.at[me], h_send.at[k], h_recv.at[me],
            device_id={"row": to}, device_id_type=MESH,
        )

    def grad_copy(owner):
        return pltpu.make_async_remote_copy(
            gcols.at[owner], cols(gr_ref, me, ff), g_send.at[owner], g_recv.at[me],
            device_id={"row": owner}, device_id_type=MESH,
        )

    def wait_shard(owner):
        pltpu.make_async_copy(og_all.at[owner], og_all.at[owner], ag_recv.at[owner]).wait()

    def forward(zp, first):
        if not first:
            wait_shard(idx(zp, y, c))

        @pl.when((zp >= z) & (z > 0))
        def _():
            down(zp).start()

        @pl.when((zp <= z) & (z < A - 1))
        def _():
            up(zp).start()

        if B > 1:
            across(zp).start()
        beside(zp, y).start()

    def forward_across(zp):
        if B > 1:
            other = (y + 1) % B
            wait_shard(idx(zp, other, c))
            beside(zp, other).start()

    own_og.wait()
    forward(z, True)
    share = -(-(n - 1) // A)

    @pl.loop(0, A)
    def _(d):
        for sign in (1, -1):
            zp = z + sign * d

            @pl.when((d > 0) & (zp >= 0) & (zp < A))
            def _():
                forward(zp, False)

        @pl.loop(0, share)
        def _(i):
            k = d * share + i + 1

            @pl.when(k < n)
            def _():
                hidden_copy(k).start()

        @pl.when(d == 0)
        def _():
            own_w.wait()
            forward_across(z)

        for sign in (1, -1):
            zp = z + sign * d

            @pl.when((d > 0) & (zp >= 0) & (zp < A))
            def _():
                forward_across(zp)

        @pl.loop(0, 4 * B)
        def _(j):
            sign = 1 - 2 * (j // (2 * B))
            r = j % (2 * B)
            zp = z + sign * d

            @pl.when((zp >= 0) & (zp < A) & ((d > 0) | (j < 2 * B)))
            def _():
                owner = idx(zp, (y + r) % B, (c + r // B) % 2)

                @pl.when(r >= B)
                def _():
                    wait_shard(owner)

                gcols[owner] = lax.dot_general(
                    og_all[owner], w_v[...], (((1,), (1,)), ((), ())),
                    preferred_element_type=jnp.float32,
                ).astype(gcols.dtype)

                @pl.when(owner == me)
                def _():
                    own_grad.start()

                @pl.when(owner != me)
                def _():
                    grad_copy(owner).start()

    own_hid.wait()

    @pl.loop(0, n)
    def _(k):
        src = (me + k) % n

        @pl.when(k > 0)
        def _():
            pltpu.make_async_copy(hid_v.at[src], hid_v.at[src], h_recv.at[src]).wait()

        hid_t[:, pl.ds(pl.multiple_of(src * rows, 128), rows)] = hid_v[src].T

    def out_copy(t):
        at = pl.ds(pl.multiple_of(t * TILE, TILE), TILE)
        return pltpu.make_async_copy(wg_v.at[:, at], wg_ref.at[:, at], out_sem.at[t])

    @pl.loop(0, depth // TILE)
    def _(t):
        at = pl.ds(pl.multiple_of(t * TILE, TILE), TILE)
        wg_v[:, at] = lax.dot_general(
            hid_t[...], og_all[:, :, at].reshape(n * rows, TILE), (((1,), (0,)), ((), ())),
            preferred_element_type=jnp.float32,
        ).astype(wg_v.dtype)
        out_copy(t).start()

    @pl.loop(0, A)
    def _(zp):
        @pl.when((zp >= z) & (z > 0))
        def _():
            down(zp).wait_send()

        @pl.when((zp <= z) & (z < A - 1))
        def _():
            up(zp).wait_send()

        if B > 1:
            across(zp).wait_send()
        for yp in range(B):
            beside(zp, yp).wait_send()

    @pl.loop(0, depth // TILE)
    def _(t):
        out_copy(t).wait()

    @pl.loop(1, n)
    def _(k):
        hidden_copy(k).wait_send()
        grad_copy((me + k) % n).wait_send()

    own_grad.wait()

    @pl.loop(1, n)
    def _(k):
        src = (me + k) % n
        pltpu.make_async_copy(cols(gr_ref, src, ff), cols(gr_ref, src, ff), g_recv.at[src]).wait()


def local(n, gate_pre, up_pre, out_grad, down_weight):
    rows, width = gate_pre.shape
    ff, depth = down_weight.shape
    B = 2 if n == 16 else 1
    A = n // (2 * B)
    flat = ff % 128 == 0
    gate_wide = gate_pre.astype(jnp.float32)
    up_wide = up_pre.astype(jnp.float32)
    hidden = (jax.nn.silu(gate_wide) * up_wide).astype(jnp.bfloat16)
    if not flat:
        hidden = hidden.reshape(rows, n, ff).transpose(1, 0, 2)
    bf16 = jnp.bfloat16
    dma = pltpu.SemaphoreType.DMA
    weight_grad, grad_rows = pl.pallas_call(
        functools.partial(kernel, A, B),
        out_shape=(
            jax.ShapeDtypeStruct((ff, depth), bf16),
            jax.ShapeDtypeStruct((rows, width) if flat else (n, rows, ff), bf16),
        ),
        in_specs=[pl.BlockSpec(memory_space=pl.ANY)] * 3,
        out_specs=(pl.BlockSpec(memory_space=pl.ANY),) * 2,
        scratch_shapes=[
            pltpu.VMEM((n, rows, depth), bf16),
            pltpu.VMEM((ff, depth), bf16),
            pltpu.VMEM((n, rows, ff), bf16),
            pltpu.VMEM((ff, n * rows), bf16),
            pltpu.VMEM((n, rows, ff), bf16),
            pltpu.VMEM((ff, depth), bf16),
            dma((4,)),
            dma((n,)),
            dma((2 * A,)),
            dma((A,)),
            dma((n // 2,)),
            dma((n,)),
            dma((n,)),
            dma((n,)),
            dma((n,)),
            dma((depth // TILE,)),
        ],
        compiler_params=pltpu.CompilerParams(
            collective_id=0, has_side_effects=True, vmem_limit_bytes=60 * 2**20
        ),
        name="swiglu_backward",
    )(hidden, out_grad, down_weight)
    if not flat:
        grad_rows = grad_rows.transpose(1, 0, 2).reshape(rows, width)
    grad_wide = grad_rows.astype(jnp.float32)
    sigmoid = 1.0 / (1.0 + jnp.exp(-gate_wide))
    up_grad = (grad_wide * gate_wide * sigmoid).astype(bf16)
    gate_grad = (grad_wide * up_wide * sigmoid * (1.0 + gate_wide * (1.0 - sigmoid))).astype(bf16)
    return (weight_grad, gate_grad, up_grad)


def solution(mesh):
    return jax.shard_map(
        functools.partial(local, mesh.shape["row"]),
        mesh=mesh,
        in_specs=(
            P(("groups", "row"), None),
            P(("groups", "row"), None),
            P(("groups", "row"), None),
            P("row", None),
        ),
        out_specs=(
            P(("groups", "row"), None),
            P(("groups", "row"), None),
            P(("groups", "row"), None),
        ),
        check_vma=False,
    )
```

time: 394 us -> 292 us (0.74)
  the two profiles are of different devices: /device:TPU:13 before, /device:TPU:30 now
where the time goes in v1:
time: 292 us
  Pallas kernels  275 us (94%)
  other arithmetic  13.3 us (5%)
  local copies, waits for them, and re-layouts  3.06 us (1%)
    pallas_call x1, Pallas kernels, local(): pl.pallas_call(functools.partial(kernel, A, B), out_shape=(jax.ShapeDtype...  275 us
    convert_element_type x1, other arithmetic, local(): up_grad = (grad_wide * gate_wide * sigmoid).astype(bf16)  7.84 us

profile of v1, /device:TPU:30, one launch (start us, length us, event | category | flops | bytes accessed | tf_op | source)
XLA Modules:
  0.0 292.1 jit_solution(5342572709925056362)
XLA Ops:
  0.6 5.5 %fusion.hid_ref = bf16[128,14336]{1,0:T(8,128)(2,1)} fusion(bf16[128,14336]{1,0:T(8,128)(2,1)} %param.5, bf16[128,14336]{1,0:T(8,128)(2,1)} %param.4), kind=kLoop, calls=%fused_computation.6 | loop fusion | flops 14680064 | bytes 11010048 | tf_op jit(solution)/shard_map/convert_element_type | solution.py:230
  6.1 0.0 copy-start
  6.1 275.1 %swiglu_backward.1 = (bf16[896,4096]{1,0:T(8,128)(2,1)}, bf16[128,14336]{1,0:T(8,128)(2,1)}) custom-call(bf16[128,14336]{1,0:T(8,128)(2,1)} %fusion.hid_ref, bf16[128,4096]{1,0:T(8,128)(2,1)} %og_ref.1, bf16[896,4096]{1,0:T(8,128)(2,1)} %w_ref.1), custom_call_target="tpu_custom_call" | custom-call | tf_op jit(solution)/shard_map/swiglu_backward/pallas_call | solution.py:235
  281.2 0.0 copy-done
  281.2 0.0 copy-start.1
  281.2 7.8 %fusion.9 = (bf16[128,14336]{1,0:T(8,128)(2,1)}, bf16[128,14336]{1,0:T(8,128)(2,1)}) fusion(bf16[128,14336]{1,0:T(8,128)(2,1)} %param.4, bf16[128,14336]{1,0:T(8,128)(2,1)} %get-tuple-element.6, bf16[128,14336]{1,0:T(8,128)(2,1)S(1)} %copy-done), kind=kLoop, calls=%fused_computation.15 | loop fusion | flops 29360128 | bytes 18350080 | tf_op jit(solution)/shard_map/convert_element_type | solution.py:270
  289.1 0.0 copy-done.1
  289.1 3.0 %copy.8 = bf16[896,4096]{1,0:T(8,128)(2,1)} copy(bf16[896,4096]{1,0:T(8,128)(2,1)S(1)} %copy-done.1) | data formatting | bytes 14680064
Async XLA Ops:
  6.1 275.1 %copy-start = (bf16[128,14336]{1,0:T(8,128)(2,1)S(1)}, bf16[128,14336]{1,0:T(8,128)(2,1)}, u32[]{:S(2)}) copy-start(bf16[128,14336]{1,0:T(8,128)(2,1)} %param.5) | copy-start | bytes 11010052
  281.2 7.9 %copy-start.1 = (bf16[896,4096]{1,0:T(8,128)(2,1)S(1)}, bf16[896,4096]{1,0:T(8,128)(2,1)}, u32[]{:S(2)}) copy-start(bf16[896,4096]{1,0:T(8,128)(2,1)} %get-tuple-element.12) | copy-start | bytes 22020100

commit v2 on v1

--- a/solution.py
+++ b/solution.py
@@ -102,65 +102,59 @@
             wait_shard(idx(zp, other, c))
             beside(zp, other).start()
 
+    def produce(zp):
+        for yp in range(B):
+            wait_shard(idx(zp, yp, 1 - c))
+        block = pl.ds(pl.multiple_of(zp * 2 * B, 2 * B), 2 * B)
+        gcols[block] = lax.dot_general(
+            og_all[block].reshape(2 * B * rows, depth), w_v[...], (((1,), (1,)), ((), ())),
+            preferred_element_type=jnp.float32,
+        ).astype(gcols.dtype).reshape(2 * B, rows, ff)
+
+        @pl.loop(0, 2 * B)
+        def _(i):
+            owner = zp * 2 * B + i
+
+            @pl.when(owner == me)
+            def _():
+                own_grad.start()
+
+            @pl.when(owner != me)
+            def _():
+                grad_copy(owner).start()
+
     own_og.wait()
     forward(z, True)
-    share = -(-(n - 1) // A)
-
-    @pl.loop(0, A)
+
+    @pl.loop(1, n)
+    def _(k):
+        hidden_copy(k).start()
+
+    own_w.wait()
+
+    @pl.loop(1, A + 1)
     def _(d):
         for sign in (1, -1):
             zp = z + sign * d
 
-            @pl.when((d > 0) & (zp >= 0) & (zp < A))
+            @pl.when((d < A) & (zp >= 0) & (zp < A))
             def _():
                 forward(zp, False)
 
-        @pl.loop(0, share)
-        def _(i):
-            k = d * share + i + 1
-
-            @pl.when(k < n)
-            def _():
-                hidden_copy(k).start()
-
-        @pl.when(d == 0)
-        def _():
-            own_w.wait()
-            forward_across(z)
-
         for sign in (1, -1):
-            zp = z + sign * d
-
-            @pl.when((d > 0) & (zp >= 0) & (zp < A))
+            zp = z + sign * (d - 1)
+
+            @pl.when(((d > 1) | (sign == 1)) & (zp >= 0) & (zp < A))
             def _():
                 forward_across(zp)
 
-        @pl.loop(0, 4 * B)
+        @pl.loop(0, 2)
         def _(j):
-            sign = 1 - 2 * (j // (2 * B))
-            r = j % (2 * B)
-            zp = z + sign * d
-
-            @pl.when((zp >= 0) & (zp < A) & ((d > 0) | (j < 2 * B)))
-            def _():
-                owner = idx(zp, (y + r) % B, (c + r // B) % 2)
-
-                @pl.when(r >= B)
-                def _():
-                    wait_shard(owner)
-
-                gcols[owner] = lax.dot_general(
-                    og_all[owner], w_v[...], (((1,), (1,)), ((), ())),
-                    preferred_element_type=jnp.float32,
-                ).astype(gcols.dtype)
-
-                @pl.when(owner == me)
-                def _():
-                    own_grad.start()
-
-                @pl.when(owner != me)
-                def _():
-                    grad_copy(owner).start()
+            zp = z + (1 - 2 * j) * (d - 1)
+
+            @pl.when(((d > 1) | (j == 0)) & (zp >= 0) & (zp < A))
+            def _():
+                produce(zp)
 
     own_hid.wait()
 

time: 292 us -> 250 us (0.86)
  the two profiles are of different devices: /device:TPU:30 before, /device:TPU:5 now
where the time goes in v2:
time: 250 us
  Pallas kernels  233 us (93%)
  other arithmetic  13.3 us (5%)
  local copies, waits for them, and re-layouts  3.06 us (1%)
    pallas_call x1, Pallas kernels, local(): pl.pallas_call(functools.partial(kernel, A, B), out_shape=(jax.ShapeDtype...  233 us
    convert_element_type x1, other arithmetic, local(): up_grad = (grad_wide * gate_wide * sigmoid).astype(bf16)  7.84 us
    convert_element_type x1, other arithmetic, local(): hidden = (jax.nn.silu(gate_wide) * up_wide).astype(jnp.bfloat16)  5.46 us

profile of v2, /device:TPU:5, one launch (start us, length us, event | category | flops | bytes accessed | tf_op | source)
XLA Modules:
  0.0 249.7 jit_solution(15304052159334687961)
XLA Ops:
  0.6 5.5 %fusion.hid_ref = bf16[128,14336]{1,0:T(8,128)(2,1)} fusion(bf16[128,14336]{1,0:T(8,128)(2,1)} %param.5, bf16[128,14336]{1,0:T(8,128)(2,1)} %param.4), kind=kLoop, calls=%fused_computation.6 | loop fusion | flops 14680064 | bytes 11010048 | tf_op jit(solution)/shard_map/convert_element_type | solution.py:224
  6.1 0.0 copy-start
  6.1 232.6 %swiglu_backward.1 = (bf16[896,4096]{1,0:T(8,128)(2,1)}, bf16[128,14336]{1,0:T(8,128)(2,1)}) custom-call(bf16[128,14336]{1,0:T(8,128)(2,1)} %fusion.hid_ref, bf16[128,4096]{1,0:T(8,128)(2,1)} %og_ref.1, bf16[896,4096]{1,0:T(8,128)(2,1)} %w_ref.1), custom_call_target="tpu_custom_call" | custom-call | tf_op jit(solution)/shard_map/swiglu_backward/pallas_call | solution.py:229
  238.7 0.0 copy-done
  238.8 0.0 copy-start.1
  238.8 7.8 %fusion.9 = (bf16[128,14336]{1,0:T(8,128)(2,1)}, bf16[128,14336]{1,0:T(8,128)(2,1)}) fusion(bf16[128,14336]{1,0:T(8,128)(2,1)} %param.4, bf16[128,14336]{1,0:T(8,128)(2,1)} %get-tuple-element.6, bf16[128,14336]{1,0:T(8,128)(2,1)S(1)} %copy-done), kind=kLoop, calls=%fused_computation.15 | loop fusion | flops 29360128 | bytes 18350080 | tf_op jit(solution)/shard_map/convert_element_type | solution.py:264
  246.6 0.0 copy-done.1
  246.6 3.0 %copy.8 = bf16[896,4096]{1,0:T(8,128)(2,1)} copy(bf16[896,4096]{1,0:T(8,128)(2,1)S(1)} %copy-done.1) | data formatting | bytes 14680064
Async XLA Ops:
  6.1 232.7 %copy-start = (bf16[128,14336]{1,0:T(8,128)(2,1)S(1)}, bf16[128,14336]{1,0:T(8,128)(2,1)}, u32[]{:S(2)}) copy-start(bf16[128,14336]{1,0:T(8,128)(2,1)} %param.5) | copy-start | bytes 11010052
  238.8 7.9 %copy-start.1 = (bf16[896,4096]{1,0:T(8,128)(2,1)S(1)}, bf16[896,4096]{1,0:T(8,128)(2,1)}, u32[]{:S(2)}) copy-start(bf16[896,4096]{1,0:T(8,128)(2,1)} %get-tuple-element.12) | copy-start | bytes 22020100

commit v3 on v2

--- a/solution.py
+++ b/solution.py
@@ -9,6 +9,9 @@
 
 MESH = pl.DeviceIdType.MESH
 TILE = 256
+PARTS = 4
+EARLY = 0
+MORE = 2
 
 
 def cols(ref, at, ff):
@@ -46,26 +49,35 @@
 
     pl.semaphore_wait(barrier, n - 1)
 
-    def shard_copy(owner, target, send):
+    part = rows // PARTS
+
+    def piece(owner, q):
+        return og_all.at[owner, pl.ds(pl.multiple_of(q * part, part), part)]
+
+    def shard_copy(owner, q, target, send):
         return pltpu.make_async_remote_copy(
-            og_all.at[owner], og_all.at[owner], send, ag_recv.at[owner],
+            piece(owner, q), piece(owner, q), send, ag_recv.at[owner * PARTS + q],
             device_id={"row": target}, device_id_type=MESH,
         )
 
-    def down(zp):
-        return shard_copy(idx(zp, y, c), idx((z + A - 1) % A, y, c), z_send.at[zp])
-
-    def up(zp):
-        return shard_copy(idx(zp, y, c), idx((z + 1) % A, y, c), z_send.at[A + zp])
-
-    def across(zp):
-        return shard_copy(idx(zp, y, c), idx(z, (y + 1) % B, c), y_send.at[zp])
-
-    def beside(zp, yp):
-        return shard_copy(idx(zp, yp, c), idx(z, y, 1 - c), c_send.at[zp * B + yp])
+    def down(zp, q):
+        return shard_copy(idx(zp, y, c), q, idx((z + A - 1) % A, y, c), z_send.at[zp * PARTS + q])
+
+    def up(zp, q):
+        return shard_copy(
+            idx(zp, y, c), q, idx((z + 1) % A, y, c), z_send.at[(A + zp) * PARTS + q]
+        )
+
+    def across(zp, q):
+        return shard_copy(idx(zp, y, c), q, idx(z, (y + 1) % B, c), y_send.at[zp * PARTS + q])
+
+    def beside(zp, yp, q):
+        return shard_copy(
+            idx(zp, yp, c), q, idx(z, y, 1 - c), c_send.at[(zp * B + yp) * PARTS + q]
+        )
 
     def hidden_copy(k):
-        to = (me + k) % n
+        to = (me + k * (7 if n % 7 else 1)) % n
         return pltpu.make_async_remote_copy(
             cols(hid_ref, to, ff), hid_v.at[me], h_send.at[k], h_recv.at[me],
             device_id={"row": to}, device_id_type=MESH,
@@ -77,34 +89,37 @@
             device_id={"row": owner}, device_id_type=MESH,
         )
 
-    def wait_shard(owner):
-        pltpu.make_async_copy(og_all.at[owner], og_all.at[owner], ag_recv.at[owner]).wait()
-
-    def forward(zp, first):
+    def wait_piece(owner, q):
+        pltpu.make_async_copy(
+            piece(owner, q), piece(owner, q), ag_recv.at[owner * PARTS + q]
+        ).wait()
+
+    def forward(zp, q, first):
         if not first:
-            wait_shard(idx(zp, y, c))
+            wait_piece(idx(zp, y, c), q)
 
         @pl.when((zp >= z) & (z > 0))
         def _():
-            down(zp).start()
+            down(zp, q).start()
 
         @pl.when((zp <= z) & (z < A - 1))
         def _():
-            up(zp).start()
+            up(zp, q).start()
 
         if B > 1:
-            across(zp).start()
-        beside(zp, y).start()
-
-    def forward_across(zp):
+            across(zp, q).start()
+        beside(zp, y, q).start()
+
+    def forward_across(zp, q):
         if B > 1:
             other = (y + 1) % B
-            wait_shard(idx(zp, other, c))
-            beside(zp, other).start()
+            wait_piece(idx(zp, other, c), q)
+            beside(zp, other, q).start()
 
     def produce(zp):
         for yp in range(B):
-            wait_shard(idx(zp, yp, 1 - c))
+            for q in range(PARTS):
+                wait_piece(idx(zp, yp, 1 - c), q)
         block = pl.ds(pl.multiple_of(zp * 2 * B, 2 * B), 2 * B)
         gcols[block] = lax.dot_general(
             og_all[block].reshape(2 * B * rows, depth), w_v[...], (((1,), (1,)), ((), ())),
@@ -124,29 +139,45 @@
                 grad_copy(owner).start()
 
     own_og.wait()
-    forward(z, True)
-
-    @pl.loop(1, n)
+
+    @pl.loop(0, PARTS)
+    def _(q):
+        forward(z, q, True)
+
+    early = min(EARLY, n - 1)
+
+    @pl.loop(1, 1 + early)
     def _(k):
         hidden_copy(k).start()
 
+    share = max(MORE, -(-(n - 1 - early) // (A * PARTS)))
     own_w.wait()
 
     @pl.loop(1, A + 1)
     def _(d):
-        for sign in (1, -1):
-            zp = z + sign * d
-
-            @pl.when((d < A) & (zp >= 0) & (zp < A))
-            def _():
-                forward(zp, False)
-
-        for sign in (1, -1):
-            zp = z + sign * (d - 1)
-
-            @pl.when(((d > 1) | (sign == 1)) & (zp >= 0) & (zp < A))
-            def _():
-                forward_across(zp)
+        @pl.loop(0, PARTS)
+        def _(q):
+            for sign in (1, -1):
+                zp = z + sign * d
+
+                @pl.when((d < A) & (zp >= 0) & (zp < A))
+                def _():
+                    forward(zp, q, False)
+
+            @pl.loop(0, share)
+            def _(i):
+                k = ((d - 1) * PARTS + q) * share + i + 1 + early
+
+                @pl.when(k < n)
+                def _():
+                    hidden_copy(k).start()
+
+            for sign in (1, -1):
+                zp = z + sign * (d - 1)
+
+                @pl.when(((d > 1) | (sign == 1)) & (zp >= 0) & (zp < A))
+                def _():
+                    forward_across(zp, q)
 
         @pl.loop(0, 2)
         def _(j):
@@ -181,20 +212,22 @@
         ).astype(wg_v.dtype)
         out_copy(t).start()
 
-    @pl.loop(0, A)
-    def _(zp):
+    @pl.loop(0, A * PARTS)
+    def _(e):
+        zp, q = e // PARTS, e % PARTS
+
         @pl.when((zp >= z) & (z > 0))
         def _():
-            down(zp).wait_send()
+            down(zp, q).wait_send()
 
         @pl.when((zp <= z) & (z < A - 1))
         def _():
-            up(zp).wait_send()
+            up(zp, q).wait_send()
 
         if B > 1:
-            across(zp).wait_send()
+            across(zp, q).wait_send()
         for yp in range(B):
-            beside(zp, yp).wait_send()
+            beside(zp, yp, q).wait_send()
 
     @pl.loop(0, depth // TILE)
     def _(t):
@@ -242,10 +275,10 @@
             pltpu.VMEM((n, rows, ff), bf16),
             pltpu.VMEM((ff, depth), bf16),
             dma((4,)),
-            dma((n,)),
-            dma((2 * A,)),
-            dma((A,)),
-            dma((n // 2,)),
+            dma((n * PARTS,)),
+            dma((2 * A * PARTS,)),
+            dma((A * PARTS,)),
+            dma((n // 2 * PARTS,)),
             dma((n,)),
             dma((n,)),
             dma((n,)),

time: 250 us -> 228 us (0.912)
  Pallas kernels: 233 us -> 211 us
    pallas_call x1, Pallas kernels: 233 us -> 211 us  [local(): pl.pallas_call(functools.partial(kernel, A, B), out_shape=(jax.ShapeDtype...]
where the time goes in v3:
time: 228 us
  Pallas kernels  211 us (93%)
  other arithmetic  13.3 us (6%)
  local copies, waits for them, and re-layouts  3.06 us (1%)
    pallas_call x1, Pallas kernels, local(): pl.pallas_call(functools.partial(kernel, A, B), out_shape=(jax.ShapeDtype...  211 us
    convert_element_type x1, other arithmetic, local(): up_grad = (grad_wide * gate_wide * sigmoid).astype(bf16)  7.84 us
    convert_element_type x1, other arithmetic, local(): hidden = (jax.nn.silu(gate_wide) * up_wide).astype(jnp.bfloat16)  5.46 us

profile of v3, /device:TPU:5, one launch (start us, length us, event | category | flops | bytes accessed | tf_op | source)
XLA Modules:
  0.0 227.8 jit_solution(7653521504480146447)
XLA Ops:
  0.6 5.5 %fusion.hid_ref = bf16[128,14336]{1,0:T(8,128)(2,1)} fusion(bf16[128,14336]{1,0:T(8,128)(2,1)} %param.5, bf16[128,14336]{1,0:T(8,128)(2,1)} %param.4), kind=kLoop, calls=%fused_computation.6 | loop fusion | flops 14680064 | bytes 11010048 | tf_op jit(solution)/shard_map/convert_element_type | solution.py:257
  6.1 0.0 copy-start
  6.1 210.8 %swiglu_backward.1 = (bf16[896,4096]{1,0:T(8,128)(2,1)}, bf16[128,14336]{1,0:T(8,128)(2,1)}) custom-call(bf16[128,14336]{1,0:T(8,128)(2,1)} %fusion.hid_ref, bf16[128,4096]{1,0:T(8,128)(2,1)} %og_ref.1, bf16[896,4096]{1,0:T(8,128)(2,1)} %w_ref.1), custom_call_target="tpu_custom_call" | custom-call | tf_op jit(solution)/shard_map/swiglu_backward/pallas_call | solution.py:262
  216.9 0.0 copy-done
  216.9 0.0 copy-start.1
  216.9 7.8 %fusion.9 = (bf16[128,14336]{1,0:T(8,128)(2,1)}, bf16[128,14336]{1,0:T(8,128)(2,1)}) fusion(bf16[128,14336]{1,0:T(8,128)(2,1)} %param.4, bf16[128,14336]{1,0:T(8,128)(2,1)} %get-tuple-element.6, bf16[128,14336]{1,0:T(8,128)(2,1)S(1)} %copy-done), kind=kLoop, calls=%fused_computation.15 | loop fusion | flops 29360128 | bytes 18350080 | tf_op jit(solution)/shard_map/convert_element_type | solution.py:297
  224.7 0.0 copy-done.1
  224.7 3.0 %copy.8 = bf16[896,4096]{1,0:T(8,128)(2,1)} copy(bf16[896,4096]{1,0:T(8,128)(2,1)S(1)} %copy-done.1) | data formatting | bytes 14680064
Async XLA Ops:
  6.1 210.8 %copy-start = (bf16[128,14336]{1,0:T(8,128)(2,1)S(1)}, bf16[128,14336]{1,0:T(8,128)(2,1)}, u32[]{:S(2)}) copy-start(bf16[128,14336]{1,0:T(8,128)(2,1)} %param.5) | copy-start | bytes 11010052
  216.9 7.9 %copy-start.1 = (bf16[896,4096]{1,0:T(8,128)(2,1)S(1)}, bf16[896,4096]{1,0:T(8,128)(2,1)}, u32[]{:S(2)}) copy-start(bf16[896,4096]{1,0:T(8,128)(2,1)} %get-tuple-element.12) | copy-start | bytes 22020100
